TPU v7x, 512 devices: a whole 4x8x8 slice. The times are simulated.
512 devices in a mesh: pp: 8 (over x, y_lo), cp: 64 (over y_hi, z, core).
Axes of the slice: x: 4, y: 8 (y_hi: 4, y_lo: 2; y = y_hi * 2 + y_lo), z: 8, core: 2. Of those that a mesh axis runs over, the one named last changes fastest.
Arguments:
- queries: bfloat16 [8, 2, 32, 4096, 128], P('pp', None, None, 'cp'), may hold values from -5 to 5
- keys_values: bfloat16 [8, 2, 2, 4, 4096, 128], P('pp', None, None, None, 'cp'), may hold values from -5 to 5
- old_block: int32 [128], replicated, may hold values from 0 to 127, as said below
- new_block: int32 [128], replicated, may hold values from 0 to 127, as said below
Outputs:
- section_input: bfloat16 [8, 2, 32, 4096, 128], P('pp', None, None, 'cp')
Inputs may be any that keep to these rules, and one draw needn't show every extreme that they name: `old_block`: A permutation of the sequence blocks; row-blocks 4 e to 4 e + 3 hold sequence blocks 2 a, 2 a + 1, 2 b, 2 b + 1 with a + b = 63. `new_block`: A permutation of the sequence blocks; row-blocks 2 d and 2 d + 1 hold sequence blocks c and 127 - c.
All inputs are finite; a program needn't handle non-finite values.
Results may differ from a plain program's by a relative error of at most 0.0098.
Values may be sent and summed in bfloat16 or wider, within the bound.
A program may use at most 64 MiB of HBM per device.

v0:
```python
import math
import jax
import jax.numpy as jnp
from jax import lax
from jax.sharding import PartitionSpec as P


def from_behind(value, axis, steps):
    count = lax.axis_size(axis)
    pairs = [(source, (source + steps) % count) for source in range(count)]
    return lax.ppermute(value, axis, pairs)


def regroup(tensor, block_order):
    dims_shape = tensor.shape
    count_blocks = block_order.shape[0]
    blocked = tensor.reshape(
        dims_shape[:-2] + (count_blocks, dims_shape[-2] // count_blocks, dims_shape[-1])
    )
    picked = jnp.take(blocked, block_order, axis=blocked.ndim - 3)
    return picked.reshape(dims_shape)


def rotate(tensor):
    half_dim = tensor.shape[-1] // 2
    spacing = jnp.arange(half_dim, dtype=jnp.float32) * (2.0 / tensor.shape[-1])
    inverse = jnp.exp(-spacing * jnp.log(jnp.float32(1000000.0)))
    angles = jnp.arange(tensor.shape[-2], dtype=jnp.float32)[:, None] * inverse[None, :]
    cosine = jnp.cos(angles)
    sine_part = jnp.sin(angles)
    widened = tensor.astype(jnp.float32)
    first_half = widened[..., :half_dim]
    second_half = widened[..., half_dim:]
    turned = jnp.concatenate(
        [
            first_half * cosine - second_half * sine_part,
            second_half * cosine + first_half * sine_part,
        ],
        axis=-1,
    )
    return turned.astype(jnp.bfloat16)


def causal_attend(queries, key_rows, value_rows):
    heads_here, length, head_width = queries.shape
    block_rows = min(512, length)
    block_count = length // block_rows
    score_scale = 1.0 / math.sqrt(head_width)
    offsets = jnp.arange(block_rows, dtype=jnp.int32)

    def query_step(query_index, finished):
        first_row = query_index * block_rows
        query_part = lax.dynamic_slice_in_dim(queries, first_row, block_rows, 1)
        query_pos = first_row + offsets

        def key_step(key_index, state_in):
            running, weight_sum, summed = state_in
            key_first = key_index * block_rows
            key_part = lax.dynamic_slice_in_dim(key_rows, key_first, block_rows, 0)
            value_part = lax.dynamic_slice_in_dim(value_rows, key_first, block_rows, 0)
            scores = (
                jnp.einsum("hqd,kd->hqk", query_part, key_part, preferred_element_type=jnp.float32)
                * score_scale
            )
            allowed = (key_first + offsets)[None, :] <= query_pos[:, None]
            scores = jnp.where(allowed[None], scores, -1e30)
            highest = jnp.maximum(running, jnp.max(scores, axis=-1))
            weights = jnp.exp(scores - highest[..., None])
            factor = jnp.exp(running - highest)
            weight_sum = weight_sum * factor + jnp.sum(weights, axis=-1)
            summed = summed * factor[..., None] + jnp.einsum(
                "hqk,kd->hqd",
                weights.astype(jnp.bfloat16),
                value_part,
                preferred_element_type=jnp.float32,
            )
            return (highest, weight_sum, summed)

        initial = (
            jnp.full((heads_here, block_rows), -1e30, jnp.float32),
            jnp.zeros((heads_here, block_rows), jnp.float32),
            jnp.zeros((heads_here, block_rows, head_width), jnp.float32),
        )
        running, weight_sum, summed = lax.fori_loop(0, query_index + 1, key_step, initial)
        output_block = (summed / weight_sum[..., None]).astype(jnp.bfloat16)
        return lax.dynamic_update_slice_in_dim(finished, output_block, first_row, 1)

    return lax.fori_loop(0, block_count, query_step, jnp.zeros(queries.shape, jnp.bfloat16))


def per_device(queries, keys_values, old_block, new_block):
    cp_devices = lax.axis_size("cp")
    sequences = queries.shape[1]
    query_heads = queries.shape[2]
    local_rows = queries.shape[3]
    head_width = queries.shape[4]
    kv_heads = keys_values.shape[3]
    all_items = sequences * query_heads
    items_here = all_items // cp_devices
    sharers = query_heads // kv_heads // items_here
    length = local_rows * cp_devices
    block_count = old_block.shape[0]
    sent_queries = queries.reshape(all_items, local_rows, head_width)
    heard_queries = lax.all_to_all(sent_queries, "cp", split_axis=0, concat_axis=1, tiled=True)
    pairs_local = keys_values.reshape(2, sequences, kv_heads, local_rows, head_width)
    copied = jnp.broadcast_to(
        pairs_local[:, :, :, None], (2, sequences, kv_heads, sharers, local_rows, head_width)
    )
    heard_pairs = lax.all_to_all(
        copied.reshape(2, cp_devices, local_rows, head_width),
        "cp",
        split_axis=1,
        concat_axis=2,
        tiled=True,
    )
    full_pairs = heard_pairs.reshape(2, length, head_width)
    positions = jnp.arange(block_count, dtype=jnp.int32)
    inverse = jnp.zeros((block_count,), jnp.int32).at[old_block].set(positions)
    query_seq = rotate(regroup(heard_queries, inverse))
    key_seq = rotate(regroup(full_pairs[0], inverse))
    value_seq = regroup(full_pairs[1], inverse)
    attended = causal_attend(query_seq, key_seq, value_seq)
    relaid = regroup(attended, new_block)
    returned_here = lax.all_to_all(relaid, "cp", split_axis=1, concat_axis=0, tiled=True)
    returned = from_behind(returned_here, "pp", 1)
    return returned.reshape(1, sequences, query_heads, local_rows, head_width)


def solution(mesh):
    return jax.shard_map(
        per_device,
        mesh=mesh,
        in_specs=(P("pp", None, None, "cp", None), P("pp", None, None, None, "cp", None), P(), P()),
        out_specs=P("pp", None, None, "cp", None),
        check_vma=False,
    )
```

profile of v0, /device:TPU:1, one launch (start us, length us, event | category | flops | bytes accessed | tf_op | source)
XLA Modules:
  0.0 305.9 jit_solution(16460065307012909908)
XLA Ops:
  0.0 17.8 %all-to-all-start = ((bf16[64,64,128]{2,1,0:T(8,128)(2,1)}), bf16[64,64,128]{2,1,0:T(8,128)(2,1)S(1)}, u32[]{:S(2)}, u32[]{:S(2)}) async-start(bf16[64,64,128]{2,1,0:T(8,128)(2,1)} %bitcast.77), calls=%async_computation | async-start | bytes 2097152 | tf_op jit(solution)/shard_map/all_to_all | solution.py:104
  17.8 31.3 %all-to-all-done = bf16[64,64,128]{2,1,0:T(8,128)(2,1)S(1)} async-done(((bf16[64,64,128]{2,1,0:T(8,128)(2,1)}), bf16[64,64,128]{2,1,0:T(8,128)(2,1)S(1)}, u32[]{:S(2)}, u32[]{:S(2)}) %all-to-all-start) | async-done | bytes 1048608 | tf_op jit(solution)/shard_map/all_to_all | solution.py:104
  49.1 1.9 broadcast_in_dim.54
  50.9 8.2 %all-to-all-start.1 = ((bf16[2,64,64,128]{3,2,0,1:T(8,128)(2,1)}), bf16[2,64,64,128]{3,2,0,1:T(8,128)(2,1)S(1)}, u32[]{:S(2)}, u32[]{:S(2)}) async-start(bf16[2,64,64,128]{3,2,0,1:T(8,128)(2,1)} %bitcast.65), calls=%async_computation.1 | async-start | bytes 4194304 | tf_op jit(solution)/shard_map/all_to_all | solution.py:109
  59.2 1.0 scatter_custom_fusion
  60.3 0.6 pad_clamp_fusion
  60.9 0.6 compare_and_fusion
  61.5 2.0 gather_fusion
  63.9 8.8 %subtract_convert_fusion.1 = (bf16[1,4096,64]{2,1,0:T(8,128)(2,1)S(1)}, bf16[1,4096,64]{2,1,0:T(8,128)(2,1)S(1)}) fusion(f32[1,4096,128]{2,1,0:T(8,128)S(1)} %bitcast_convert_fusion.1, f32[64]{0:T(128)S(1)} %multiply_exponential_fusion), kind=kLoop, calls=%fused_computation.33 | loop fusion | flops 2359296 | bytes 3145984 | tf_op jit(solution)/shard_map/convert.4
  72.6 1.5 pad_maximum_fusion
  74.2 52.6 %all-to-all-done.1 = bf16[2,64,64,128]{3,2,0,1:T(8,128)(2,1)S(1)} async-done(((bf16[2,64,64,128]{3,2,0,1:T(8,128)(2,1)}), bf16[2,64,64,128]{3,2,0,1:T(8,128)(2,1)S(1)}, u32[]{:S(2)}, u32[]{:S(2)}) %all-to-all-start.1) | async-done | bytes 2097184 | tf_op jit(solution)/shard_map/all_to_all | solution.py:109
  126.8 1.2 fusion.22
  127.9 0.8 gather_fusion.1
  128.7 0.5 copy-done.1
  129.1 0.8 gather_fusion.2
  130.4 8.6 %subtract_convert_fusion = (bf16[4096,64]{1,0:T(8,128)(2,1)S(1)}, bf16[4096,64]{1,0:T(8,128)(2,1)S(1)}) fusion(f32[4096,128]{1,0:T(8,128)S(1)} %bitcast_convert_fusion, f32[64]{0:T(128)S(1)} %multiply_exponential_fusion), kind=kLoop, calls=%fused_computation.28 | loop fusion | flops 2359296 | bytes 3145984 | tf_op jit(solution)/shard_map/convert.2
  139.0 0.6 pad_maximum_fusion.1
  139.8 45.7 %while.48 = (s32[]{:T(128)}, bf16[1,4096,128]{2,1,0:T(8,128)(2,1)S(1)}, bf16[1,4096,128]{2,1,0:T(8,128)(2,1)}, bf16[4096,128]{1,0:T(8,128)(2,1)S(1)}, bf16[4096,...) while((s32[]{:T(128)}, ...), condition=%wide.region_6.0_spmd.clone.clone, body=%wide.region_1.8_spmd.clone.clone.sunk | while | flops 136579072 | bytes 5032458 | solution.py:88
  139.8 0.9 constant_dynamic-slice_fusion.2
  140.8 1.0 while.49
  142.0 0.9 constant_dynamic-slice_fusion.2
  143.0 2.0 while.49
  144.6 0.4 fusion.34
  145.2 0.9 constant_dynamic-slice_fusion.2
  146.2 3.0 while.49
  148.8 0.4 fusion.34
  149.4 0.9 constant_dynamic-slice_fusion.2
  150.4 4.0 %while.49 = (s32[]{:T(128)}, f32[1,512]{1,0:T(1,128)S(1)}, f32[1,512]{1,0:T(1,128)S(1)}, f32[1,512,128]{2,1,0:T(8,128)S(1)}, s32[]{:T(128)}, /*index=5*/s32[512]...) while((s32[]{:T(128)}, f32[1,512]{1,0:T(1,128)S(1)}, ...), condition=%wide.region_5.7_spmd, body=%wide.region_2.6_spmd.sunk | while | flops 136447488 | bytes 4104383 | solution.py:84
  153.0 0.4 fusion.34
  154.0 0.4 fusion.34
  154.6 0.9 constant_dynamic-slice_fusion.2
  155.6 5.0 %while.49 = (s32[]{:T(128)}, f32[1,512]{1,0:T(1,128)S(1)}, f32[1,512]{1,0:T(1,128)S(1)}, f32[1,512,128]{2,1,0:T(8,128)S(1)}, s32[]{:T(128)}, /*index=5*/s32[512]...) while((s32[]{:T(128)}, f32[1,512]{1,0:T(1,128)S(1)}, ...), condition=%wide.region_5.7_spmd, body=%wide.region_2.6_spmd.sunk | while | flops 136447488 | bytes 4104383 | solution.py:84
  158.2 0.4 fusion.34
  159.2 0.4 fusion.34
  160.2 0.4 fusion.34
  160.8 0.9 constant_dynamic-slice_fusion.2
  161.8 6.0 %while.49 = (s32[]{:T(128)}, f32[1,512]{1,0:T(1,128)S(1)}, f32[1,512]{1,0:T(1,128)S(1)}, f32[1,512,128]{2,1,0:T(8,128)S(1)}, s32[]{:T(128)}, /*index=5*/s32[512]...) while((s32[]{:T(128)}, f32[1,512]{1,0:T(1,128)S(1)}, ...), condition=%wide.region_5.7_spmd, body=%wide.region_2.6_spmd.sunk | while | flops 136447488 | bytes 4104383 | solution.py:84
  164.4 0.4 fusion.34
  165.4 0.4 fusion.34
  166.4 0.4 fusion.34
  167.4 0.4 fusion.34
  168.0 0.9 constant_dynamic-slice_fusion.2
  169.0 7.0 %while.49 = (s32[]{:T(128)}, f32[1,512]{1,0:T(1,128)S(1)}, f32[1,512]{1,0:T(1,128)S(1)}, f32[1,512,128]{2,1,0:T(8,128)S(1)}, s32[]{:T(128)}, /*index=5*/s32[512]...) while((s32[]{:T(128)}, f32[1,512]{1,0:T(1,128)S(1)}, ...), condition=%wide.region_5.7_spmd, body=%wide.region_2.6_spmd.sunk | while | flops 136447488 | bytes 4104383 | solution.py:84
  171.6 0.4 fusion.34
  172.6 0.4 fusion.34
  173.6 0.4 fusion.34
  174.6 0.4 fusion.34
  175.6 0.4 fusion.34
  176.2 0.9 constant_dynamic-slice_fusion.2
  177.2 8.0 %while.49 = (s32[]{:T(128)}, f32[1,512]{1,0:T(1,128)S(1)}, f32[1,512]{1,0:T(1,128)S(1)}, f32[1,512,128]{2,1,0:T(8,128)S(1)}, s32[]{:T(128)}, /*index=5*/s32[512]...) while((s32[]{:T(128)}, f32[1,512]{1,0:T(1,128)S(1)}, ...), condition=%wide.region_5.7_spmd, body=%wide.region_2.6_spmd.sunk | while | flops 136447488 | bytes 4104383 | solution.py:84
  179.8 0.4 fusion.34
  180.8 0.4 fusion.34
  181.8 0.4 fusion.34
  182.8 0.4 fusion.34
  183.8 0.4 fusion.34
  185.4 0.9 gather_fusion.3
  186.6 16.7 %copy.10 = bf16[1,4096,128]{2,0,1:T(2,128)(2,1)S(1)} copy(bf16[1,4096,128]{2,1,0:T(8,128)(2,1)S(1)} %bitcast.69) | data formatting | bytes 2097152 | tf_op jit(solution)/shard_map/reshape | solution.py:21
  203.3 0.5 broadcast.145
  203.8 22.4 %reduce.4 = bf16[4096,128]{1,0:T(8,128)(2,1)S(1)} reduce(bf16[4096,1,128]{2,1,0:T(2,128)(2,1)S(1)} %bitcast.66, bf16[]{:T(256)} %broadcast.145), dimensions={1}, to_apply=%bitcast.46.reduce_sub_computation | reduce | bytes 2097154
  226.5 48.5 %all_to_all.30 = bf16[64,2,4096]{2,1,0:T(2,128)(2,1)S(1)} all-to-all(bf16[64,2,4096]{2,1,0:T(2,128)(2,1)S(1)} %reshape.272), channel_id=1, replica_groups=mesh['pp'=8,'cp'=64] {'cp'}, dimensions={0} | all-to-all | bytes 2097152 | tf_op jit(solution)/shard_map/all_to_all | solution.py:124
  275.0 1.0 reshape.273
  276.2 1.9 collective-permute-start
  278.2 26.8 %collective-permute-done = bf16[64,64,128]{2,1,0:T(8,128)(2,1)S(1)} collective-permute-done((bf16[64,64,128]{2,1,0:T(8,128)(2,1)S(1)}, bf16[64,64,128]{2,1,0:T(8,128)(2,1)S(1)}, u32[]{:S(2)}, u32[]{:S(2)}) %collective-permute-start) | collective-permute-done | bytes 1048608 | tf_op jit(solution)/shard_map/ppermute | solution.py:11
  305.0 1.0 copy.33
  (306 shorter events, 29.1 us)
Async XLA Ops:
  0.0 17.8 %copy-start.2 = (bf16[1,2,2,4,64,128]{5,4,3,2,1,0:T(8,128)(2,1)S(1)}, bf16[1,2,2,4,64,128]{5,4,3,2,1,0:T(8,128)(2,1)}, u32[]{:S(2)}) copy-start(bf16[1,2,2,4,64,128]{5,4,3,2,1,0:T(8,128)(2,1)} %param.13) | copy-start | bytes 786436
  0.0 49.1 %all-to-all-start = ((bf16[64,64,128]{2,1,0:T(8,128)(2,1)}), bf16[64,64,128]{2,1,0:T(8,128)(2,1)S(1)}, u32[]{:S(2)}, u32[]{:S(2)}) async-start(bf16[64,64,128]{2,1,0:T(8,128)(2,1)} %bitcast.77), calls=%async_computation | async-start | bytes 2097152 | tf_op jit(solution)/shard_map/all_to_all | solution.py:104
  49.1 1.9 copy-start
  50.9 8.3 %copy-start.4 = (s32[128]{0:T(128)S(1)}, s32[128]{0:T(128)}, u32[]{:S(2)}) copy-start(s32[128]{0:T(128)} %param.14) | copy-start | bytes 1540
  50.9 9.3 %copy-start.5 = (s32[128]{0:T(128)S(1)}, s32[128]{0:T(128)}, u32[]{:S(2)}) copy-start(s32[128]{0:T(128)} %param.15) | copy-start | bytes 1540
  50.9 75.8 %all-to-all-start.1 = ((bf16[2,64,64,128]{3,2,0,1:T(8,128)(2,1)}), bf16[2,64,64,128]{3,2,0,1:T(8,128)(2,1)S(1)}, u32[]{:S(2)}, u32[]{:S(2)}) async-start(bf16[2,64,64,128]{3,2,0,1:T(8,128)(2,1)} %bitcast.65), calls=%async_computation.1 | async-start | bytes 4194304 | tf_op jit(solution)/shard_map/all_to_all | solution.py:109
  127.9 1.2 copy-start.1
  185.4 0.9 copy-start.3
  276.2 28.7 %collective-permute-start = (bf16[64,64,128]{2,1,0:T(8,128)(2,1)S(1)}, bf16[64,64,128]{2,1,0:T(8,128)(2,1)S(1)}, u32[]{:S(2)}, u32[]{:S(2)}) collective-permute-start(bf16[64,64,128]{2,1,0:T(8,128)(2,1)S(1)} %bitcast.76), channel_id=1, source_target_pairs={{0,64},{64,128},{128,192},{192,256},{256,320},{320,384},{384,448},... | collective-permute-start | bytes 3145736 | tf_op jit(solution)/shard_map/ppermute | solution.py:11
where the time goes:
time: 307 us; the launch traced here: 306 us
  waiting for transfers between devices  111 us (36%)
  other arithmetic  53.7 us (17%)
  blocking collectives  48.5 us (16%)
  local copies, waits for them, and re-layouts  36.4 us (12%)
  starting transfers between devices  27.9 us (9%)
  matrix products  25.8 us (8%)
    all_to_all x1, waiting for transfers between devices, per_device(): lax.all_to_all(copied.reshape(2, cp_devices, local_rows, head_width), 'cp...  52.6 us
    all_to_all x1, blocking collectives, per_device(): lax.all_to_all(relaid, 'cp', split_axis=1, concat_axis=0, tiled=True)  48.5 us
    all_to_all x1, waiting for transfers between devices, per_device(): lax.all_to_all(sent_queries, 'cp', split_axis=0, concat_axis=1, tiled=True)  31.3 us
    ppermute x1, waiting for transfers between devices, from_behind(): return lax.ppermute(value, axis, pairs)  26.8 us
    unnamed x1, other arithmetic  22.4 us
    all_to_all x1, starting transfers between devices, per_device(): lax.all_to_all(sent_queries, 'cp', split_axis=0, concat_axis=1, tiled=True)  17.8 us
    another operation x2, other arithmetic  17.3 us
    reshape x1, local copies, waits for them, and re-layouts, regroup(): return picked.reshape(dims_shape)  16.7 us
  transfers between devices with their start and end apart: 3, of which 3 were waited for; matrix products, arithmetic and copies ran while one was open for 5% of the time, Pallas kernels for 0%

commit v1 on v0

--- a/solution.py
+++ b/solution.py
@@ -3,6 +3,16 @@
 import jax.numpy as jnp
 from jax import lax
 from jax.sharding import PartitionSpec as P
+
+time_packet = lambda here_x: jnp.concatenate(
+    jax.lax.all_to_all(
+        jnp.stack(jnp.split(here_x, jax.lax.axis_size("cp"), axis=1), axis=0),
+        split_axis=0,
+        axis_name="cp",
+        concat_axis=0,
+    ),
+    axis=0,
+)
 
 
 def from_behind(value, axis, steps):
@@ -121,7 +131,7 @@
     value_seq = regroup(full_pairs[1], inverse)
     attended = causal_attend(query_seq, key_seq, value_seq)
     relaid = regroup(attended, new_block)
-    returned_here = lax.all_to_all(relaid, "cp", split_axis=1, concat_axis=0, tiled=True)
+    returned_here = time_packet(relaid)
     returned = from_behind(returned_here, "pp", 1)
     return returned.reshape(1, sequences, query_heads, local_rows, head_width)
 

time: 307 us -> 267 us (0.87)
  other arithmetic: 53.7 us -> 32.3 us
  local copies, waits for them, and re-layouts: 36.4 us -> 18.7 us
    unnamed x1 -> x0, other arithmetic: 22.4 us -> none
    reshape x1 -> x0, local copies, waits for them, and re-layouts: 16.7 us -> none  [regroup(): return picked.reshape(dims_shape)]
  transfers between devices with their start and end apart: 3 -> 3, of which waited for: 3 -> 3; matrix products, arithmetic and copies ran while one was open for 5% -> 6% of each run, Pallas kernels for 0% -> 0%
where the time goes in v1:
time: 267 us; the launch traced here: 266 us
  waiting for transfers between devices  110 us (41%)
  blocking collectives  48.7 us (18%)
  other arithmetic  32.3 us (12%)
  starting transfers between devices  27.9 us (10%)
  matrix products  25.8 us (10%)
  local copies, waits for them, and re-layouts  18.7 us (7%)
  loops' own time  2.67 us (1%)
    all_to_all x1, waiting for transfers between devices, per_device(): lax.all_to_all(copied.reshape(2, cp_devices, local_rows, head_width), 'cp...  51.8 us
    all_to_all x1, blocking collectives, jax.lax.all_to_all(jnp.stack(jnp.split(here_x, jax.lax.axis_size('cp'), a...  48.7 us
    all_to_all x1, waiting for transfers between devices, per_device(): lax.all_to_all(sent_queries, 'cp', split_axis=0, concat_axis=1, tiled=True)  31.3 us
    ppermute x1, waiting for transfers between devices, from_behind(): return lax.ppermute(value, axis, pairs)  26.8 us
    all_to_all x1, starting transfers between devices, per_device(): lax.all_to_all(sent_queries, 'cp', split_axis=0, concat_axis=1, tiled=True)  17.8 us
    another operation x2, other arithmetic  17.2 us
    dot_general x36, matrix products, key_step(): jnp.einsum('hqk,kd->hqd', weights.astype(jnp.bfloat16), value_part, prefe...  14.2 us
    dot_general x36, matrix products, key_step(): jnp.einsum('hqd,kd->hqk', query_part, key_part, preferred_element_type=jn...  11.6 us
  transfers between devices with their start and end apart: 3, of which 3 were waited for; matrix products, arithmetic and copies ran while one was open for 6% of the time, Pallas kernels for 0%

profile of v1, /device:TPU:1, one launch (start us, length us, event | category | flops | bytes accessed | tf_op | source)
XLA Modules:
  0.0 266.5 jit_solution(16452215905135708340)
XLA Ops:
  0.0 17.8 %all-to-all-start = ((bf16[64,64,128]{2,1,0:T(8,128)(2,1)}), bf16[64,64,128]{2,1,0:T(8,128)(2,1)S(1)}, u32[]{:S(2)}, u32[]{:S(2)}) async-start(bf16[64,64,128]{2,1,0:T(8,128)(2,1)} %bitcast.389), calls=%async_computation | async-start | bytes 2097152 | tf_op jit(solution)/shard_map/all_to_all | solution.py:114
  17.8 31.3 %all-to-all-done = bf16[64,64,128]{2,1,0:T(8,128)(2,1)S(1)} async-done(((bf16[64,64,128]{2,1,0:T(8,128)(2,1)}), bf16[64,64,128]{2,1,0:T(8,128)(2,1)S(1)}, u32[]{:S(2)}, u32[]{:S(2)}) %all-to-all-start) | async-done | bytes 1048608 | tf_op jit(solution)/shard_map/all_to_all | solution.py:114
  49.1 1.9 broadcast_in_dim.54
  50.9 8.2 %all-to-all-start.1 = ((bf16[2,64,64,128]{3,2,0,1:T(8,128)(2,1)}), bf16[2,64,64,128]{3,2,0,1:T(8,128)(2,1)S(1)}, u32[]{:S(2)}, u32[]{:S(2)}) async-start(bf16[2,64,64,128]{3,2,0,1:T(8,128)(2,1)} %bitcast.316), calls=%async_computation.1 | async-start | bytes 4194304 | tf_op jit(solution)/shard_map/all_to_all | solution.py:119
  59.2 1.0 scatter_custom_fusion
  60.3 0.6 pad_clamp_fusion
  60.9 0.6 compare_and_fusion
  61.5 1.7 gather_fusion
  63.1 1.4 bitcast_select_fusion.1
  64.8 8.6 %subtract_convert_fusion.1 = (bf16[1,4096,64]{2,1,0:T(8,128)(2,1)S(1)}, bf16[1,4096,64]{2,1,0:T(8,128)(2,1)S(1)}) fusion(f32[1,4096,128]{2,1,0:T(8,128)S(1)} %bitcast_convert_fusion.1, f32[64]{0:T(128)S(1)} %multiply_exponential_fusion), kind=kLoop, calls=%fused_computation.33 | loop fusion | flops 2359296 | bytes 3145984 | tf_op jit(solution)/shard_map/convert.4
  73.3 1.6 pad_maximum_fusion
  74.9 51.8 %all-to-all-done.1 = bf16[2,64,64,128]{3,2,0,1:T(8,128)(2,1)S(1)} async-done(((bf16[2,64,64,128]{3,2,0,1:T(8,128)(2,1)}), bf16[2,64,64,128]{3,2,0,1:T(8,128)(2,1)S(1)}, u32[]{:S(2)}, u32[]{:S(2)}) %all-to-all-start.1) | async-done | bytes 2097184 | tf_op jit(solution)/shard_map/all_to_all | solution.py:119
  126.7 1.2 fusion.22
  127.9 2.0 gather_fusion.1
  129.9 0.8 gather_fusion.2
  131.2 8.6 %subtract_convert_fusion = (bf16[4096,64]{1,0:T(8,128)(2,1)S(1)}, bf16[4096,64]{1,0:T(8,128)(2,1)S(1)}) fusion(f32[4096,128]{1,0:T(8,128)S(1)} %bitcast_convert_fusion, f32[64]{0:T(128)S(1)} %multiply_exponential_fusion), kind=kLoop, calls=%fused_computation.28 | loop fusion | flops 2359296 | bytes 3145984 | tf_op jit(solution)/shard_map/convert.2
  139.7 0.6 pad_maximum_fusion.1
  140.5 45.6 %while.48 = (s32[]{:T(128)}, bf16[1,4096,128]{2,1,0:T(8,128)(2,1)S(1)}, bf16[1,4096,128]{2,1,0:T(8,128)(2,1)}, bf16[4096,128]{1,0:T(8,128)(2,1)S(1)}, bf16[4096,...) while((s32[]{:T(128)}, ...), condition=%wide.region_6.0_spmd.clone.clone, body=%wide.region_1.8_spmd.clone.clone.sunk | while | flops 136579072 | bytes 5032458 | solution.py:98
  140.5 0.9 constant_dynamic-slice_fusion.2
  141.5 1.0 while.49
  142.1 0.4 fusion.34
  142.7 0.9 constant_dynamic-slice_fusion.2
  143.7 2.0 while.49
  144.3 0.4 fusion.34
  145.3 0.4 fusion.34
  145.9 0.9 constant_dynamic-slice_fusion.2
  146.9 3.0 %while.49 = (s32[]{:T(128)}, f32[1,512]{1,0:T(1,128)S(1)}, f32[1,512]{1,0:T(1,128)S(1)}, f32[1,512,128]{2,1,0:T(8,128)S(1)}, s32[]{:T(128)}, /*index=5*/s32[512]...) while((s32[]{:T(128)}, f32[1,512]{1,0:T(1,128)S(1)}, ...), condition=%wide.region_5.7_spmd, body=%wide.region_2.6_spmd.sunk | while | flops 136447488 | bytes 4104383 | solution.py:94
  148.5 0.4 fusion.34
  149.5 0.4 fusion.34
  150.1 0.9 constant_dynamic-slice_fusion.2
  151.1 4.0 %while.49 = (s32[]{:T(128)}, f32[1,512]{1,0:T(1,128)S(1)}, f32[1,512]{1,0:T(1,128)S(1)}, f32[1,512,128]{2,1,0:T(8,128)S(1)}, s32[]{:T(128)}, /*index=5*/s32[512]...) while((s32[]{:T(128)}, f32[1,512]{1,0:T(1,128)S(1)}, ...), condition=%wide.region_5.7_spmd, body=%wide.region_2.6_spmd.sunk | while | flops 136447488 | bytes 4104383 | solution.py:94
  152.7 0.4 fusion.34
  154.7 0.4 fusion.34
  155.3 0.9 constant_dynamic-slice_fusion.2
  156.3 5.0 %while.49 = (s32[]{:T(128)}, f32[1,512]{1,0:T(1,128)S(1)}, f32[1,512]{1,0:T(1,128)S(1)}, f32[1,512,128]{2,1,0:T(8,128)S(1)}, s32[]{:T(128)}, /*index=5*/s32[512]...) while((s32[]{:T(128)}, f32[1,512]{1,0:T(1,128)S(1)}, ...), condition=%wide.region_5.7_spmd, body=%wide.region_2.6_spmd.sunk | while | flops 136447488 | bytes 4104383 | solution.py:94
  157.9 0.4 fusion.34
  159.9 0.4 fusion.34
  160.9 0.4 fusion.34
  161.5 0.9 constant_dynamic-slice_fusion.2
  162.5 6.0 %while.49 = (s32[]{:T(128)}, f32[1,512]{1,0:T(1,128)S(1)}, f32[1,512]{1,0:T(1,128)S(1)}, f32[1,512,128]{2,1,0:T(8,128)S(1)}, s32[]{:T(128)}, /*index=5*/s32[512]...) while((s32[]{:T(128)}, f32[1,512]{1,0:T(1,128)S(1)}, ...), condition=%wide.region_5.7_spmd, body=%wide.region_2.6_spmd.sunk | while | flops 136447488 | bytes 4104383 | solution.py:94
  164.1 0.4 fusion.34
  166.1 0.4 fusion.34
  167.1 0.4 fusion.34
  168.1 0.4 fusion.34
  168.7 0.9 constant_dynamic-slice_fusion.2
  169.7 7.0 %while.49 = (s32[]{:T(128)}, f32[1,512]{1,0:T(1,128)S(1)}, f32[1,512]{1,0:T(1,128)S(1)}, f32[1,512,128]{2,1,0:T(8,128)S(1)}, s32[]{:T(128)}, /*index=5*/s32[512]...) while((s32[]{:T(128)}, f32[1,512]{1,0:T(1,128)S(1)}, ...), condition=%wide.region_5.7_spmd, body=%wide.region_2.6_spmd.sunk | while | flops 136447488 | bytes 4104383 | solution.py:94
  171.3 0.4 fusion.34
  173.3 0.4 fusion.34
  174.3 0.4 fusion.34
  175.3 0.4 fusion.34
  176.3 0.4 fusion.34
  176.9 0.9 constant_dynamic-slice_fusion.2
  177.9 8.0 %while.49 = (s32[]{:T(128)}, f32[1,512]{1,0:T(1,128)S(1)}, f32[1,512]{1,0:T(1,128)S(1)}, f32[1,512,128]{2,1,0:T(8,128)S(1)}, s32[]{:T(128)}, /*index=5*/s32[512]...) while((s32[]{:T(128)}, f32[1,512]{1,0:T(1,128)S(1)}, ...), condition=%wide.region_5.7_spmd, body=%wide.region_2.6_spmd.sunk | while | flops 136447488 | bytes 4104383 | solution.py:94
  179.5 0.4 fusion.34
  181.5 0.4 fusion.34
  182.5 0.4 fusion.34
  183.5 0.4 fusion.34
  184.5 0.4 fusion.34
  185.5 0.4 fusion.34
  186.1 0.9 gather_fusion.3
  188.0 48.7 %all_to_all.23 = bf16[64,1,64,128]{3,2,1,0:T(8,128)(2,1)S(1)} all-to-all(bf16[64,1,64,128]{3,2,1,0:T(8,128)(2,1)S(1)} %constant_dynamic-update-slice_fusion), channel_id=1, replica_groups=mesh['pp'=8,'cp'=64] {'cp'}, dimensions={0} | all-to-all | bytes 2097152 | tf_op jit(solution)/shard_map/all_to_all | solution.py:8
  236.8 1.9 collective-permute-start
  238.7 26.8 %collective-permute-done = bf16[64,64,128]{2,1,0:T(8,128)(2,1)S(1)} collective-permute-done((bf16[64,64,128]{2,1,0:T(8,128)(2,1)S(1)}, bf16[64,64,128]{2,1,0:T(8,128)(2,1)S(1)}, u32[]{:S(2)}, u32[]{:S(2)}) %collective-permute-start) | collective-permute-done | bytes 1048608 | tf_op jit(solution)/shard_map/ppermute | solution.py:21
  265.5 1.0 copy.154
  (360 shorter events, 27.4 us)
Async XLA Ops:
  0.0 17.8 %copy-start = (bf16[1,2,2,4,64,128]{5,4,3,2,1,0:T(8,128)(2,1)S(1)}, bf16[1,2,2,4,64,128]{5,4,3,2,1,0:T(8,128)(2,1)}, u32[]{:S(2)}) copy-start(bf16[1,2,2,4,64,128]{5,4,3,2,1,0:T(8,128)(2,1)} %param.13) | copy-start | bytes 786436
  0.0 49.1 %all-to-all-start = ((bf16[64,64,128]{2,1,0:T(8,128)(2,1)}), bf16[64,64,128]{2,1,0:T(8,128)(2,1)S(1)}, u32[]{:S(2)}, u32[]{:S(2)}) async-start(bf16[64,64,128]{2,1,0:T(8,128)(2,1)} %bitcast.389), calls=%async_computation | async-start | bytes 2097152 | tf_op jit(solution)/shard_map/all_to_all | solution.py:114
  50.9 8.3 %copy-start.2 = (s32[128]{0:T(128)S(1)}, s32[128]{0:T(128)}, u32[]{:S(2)}) copy-start(s32[128]{0:T(128)} %param.14) | copy-start | bytes 1540
  50.9 9.3 %copy-start.3 = (s32[128]{0:T(128)S(1)}, s32[128]{0:T(128)}, u32[]{:S(2)}) copy-start(s32[128]{0:T(128)} %param.15) | copy-start | bytes 1540
  50.9 75.8 %all-to-all-start.1 = ((bf16[2,64,64,128]{3,2,0,1:T(8,128)(2,1)}), bf16[2,64,64,128]{3,2,0,1:T(8,128)(2,1)S(1)}, u32[]{:S(2)}, u32[]{:S(2)}) async-start(bf16[2,64,64,128]{3,2,0,1:T(8,128)(2,1)} %bitcast.316), calls=%async_computation.1 | async-start | bytes 4194304 | tf_op jit(solution)/shard_map/all_to_all | solution.py:119
  186.1 0.9 copy-start.1
  236.8 28.7 %collective-permute-start = (bf16[64,64,128]{2,1,0:T(8,128)(2,1)S(1)}, bf16[64,64,128]{2,1,0:T(8,128)(2,1)S(1)}, u32[]{:S(2)}, u32[]{:S(2)}) collective-permute-start(bf16[64,64,128]{2,1,0:T(8,128)(2,1)S(1)} %bitcast.390), channel_id=1, source_target_pairs={{0,64},{64,128},{128,192},{192,256},{256,320},{320,384},{384,448},... | collective-permute-start | bytes 3145736 | tf_op jit(solution)/shard_map/ppermute | solution.py:21
